TPU v7x, 512 devices: a whole 4x4x16 slice. The times are simulated.
512 devices in a mesh: dp: 128 (over x, z, core), tensor: 4 (over y).
Axes of the slice: x: 4, y: 4, z: 16, core: 2. Of those that a mesh axis runs over, the one named last changes fastest.
Arguments:
- tokens: bfloat16 [32768, 2048], P('dp', 'tensor'), may hold values from -6 to 6
- expert_ids: int32 [32768, 2], P('dp'), may hold values from 0 to 127, as said below
- route_weights: float32 [32768, 2], P('dp'), may hold values from 0.2 to 1
- gate_weight: bfloat16 [128, 2048, 1024], P('dp', None, 'tensor'), may hold values from -0.125 to 0.125
- up_weight: bfloat16 [128, 2048, 1024], P('dp', None, 'tensor'), may hold values from -0.125 to 0.125
- down_weight: bfloat16 [128, 1024, 2048], P('dp', 'tensor'), may hold values from -0.1875 to 0.1875
Outputs:
- moe_out: bfloat16 [32768, 2048], P('dp', 'tensor')
Inputs may be any that keep to these rules, and one draw needn't show every extreme that they name: `expert_ids`: the two experts of a row differ. Among the rows of one index of dp, no expert is named more than 8 times.
All inputs are finite; a program needn't handle non-finite values.
Results may differ from a plain program's by a relative error of at most 0.011.
Values may be sent and summed in bfloat16 or wider, within the bound.
A program may use at most 64 MiB of HBM per device.

v0:
```python
import jax
import jax.numpy as jnp
from jax import lax
from jax.sharding import PartitionSpec as P


def body(tokens, expert_ids, route_weights, gate_weight, up_weight, down_weight):
    tok_count = tokens.shape[0]
    local_experts = gate_weight.shape[0]
    model_width = gate_weight.shape[1]
    groups = lax.axis_size("dp")
    experts_all = local_experts * groups
    capacity = 4 * tok_count // groups
    chosen = expert_ids.reshape(-1)
    onehot = (chosen[:, None] == jnp.arange(experts_all, dtype=jnp.int32)[None, :]).astype(
        jnp.int32
    )
    earlier = jnp.cumsum(onehot, axis=0) - onehot
    slot_index = jnp.sum(earlier * onehot, axis=1)
    flat_slot = chosen * capacity + slot_index
    source_rows = tokens[jnp.arange(chosen.shape[0], dtype=jnp.int32) // 2]
    send_buffer = (
        jnp.zeros((experts_all * capacity, tokens.shape[1]), jnp.bfloat16)
        .at[flat_slot]
        .set(source_rows)
    )
    send_buffer = send_buffer.reshape(experts_all, 1, capacity, tokens.shape[1])
    features = lax.all_gather(
        lax.all_to_all(send_buffer, "dp", split_axis=0, concat_axis=1, tiled=True),
        "tensor",
        axis=3,
        tiled=True,
    )
    slot_count = features.shape[2]
    token_rows = features[0].reshape(-1, model_width)
    gate_value = jnp.dot(token_rows, gate_weight[0], preferred_element_type=jnp.float32)
    up_value = jnp.dot(token_rows, up_weight[0], preferred_element_type=jnp.float32)
    hidden = (jax.nn.silu(gate_value) * up_value).astype(jnp.bfloat16)
    partial_sum = jnp.dot(hidden, down_weight[0], preferred_element_type=jnp.float32)
    results = [partial_sum.reshape(features.shape[1], slot_count, model_width)]
    partial_out = jnp.stack(results, axis=0)
    reduced = lax.psum_scatter(
        partial_out.astype(jnp.bfloat16), "tensor", scatter_dimension=3, tiled=True
    )
    came_back = lax.all_to_all(reduced, "dp", split_axis=1, concat_axis=0, tiled=True)
    quarter_width = came_back.shape[3]
    result_table = came_back.reshape(experts_all * capacity, quarter_width)
    picked = result_table[flat_slot].astype(jnp.float32).reshape(tok_count, 2, quarter_width)
    mixed_out = jnp.sum(picked * route_weights[:, :, None], axis=1)
    return mixed_out.astype(jnp.bfloat16)


def solution(mesh):
    return jax.shard_map(
        body,
        mesh=mesh,
        in_specs=(
            P("dp", "tensor"),
            P("dp", None),
            P("dp", None),
            P("dp", None, "tensor"),
            P("dp", None, "tensor"),
            P("dp", "tensor", None),
        ),
        out_specs=P("dp", "tensor"),
        check_vma=False,
    )
```

profile of v0, /device:TPU:1, one launch (start us, length us, event | category | flops | bytes accessed | tf_op | source)
XLA Modules:
  0.0 288.6 jit_solution(14001448226767223536)
XLA Ops:
  6.5 0.0 copy-start
  6.5 0.0 copy-start.3
  6.5 0.0 all-gather.3.cloned.1.call-start
  6.5 1.0 copy.18
  7.5 0.1 eq.29
  7.7 0.1 eq.25
  7.8 0.7 broadcast_multiply_fusion
  8.5 0.1 copy.20
  8.6 0.2 fusion.22
  8.9 0.1 copy.17
  9.1 0.1 mul.36
  9.2 0.2 fusion.21
  9.5 6.4 %scatter_custom_fusion = bf16[1024,512]{1,0:T(8,128)(2,1)S(1)} fusion(s32[512]{0:T(512)S(1)} %bitcast.49, bf16[256,512]{1,0:T(8,128)(2,1)} %param.6, s32[1024]{0:T(1024)S(1)} %pad_clamp_fusion.1, bf16[]{:T(256)} %constant.26.clone.1), kind=kCustom, calls=%fused_computation.16 | custom fusion | bytes 1049088 | tf_op jit(solution)/shard_map/scatter | solution.py:25
  15.9 74.7 %all_to_all.21 = bf16[128,1,8,512]{3,2,1,0:T(8,128)(2,1)} all-to-all(bf16[128,1,8,512]{3,2,1,0:T(8,128)(2,1)S(1)} %bitcast.44), channel_id=1, replica_groups=mesh['dp'=128,'tensor'=4] {'dp'}, dimensions={0} | all-to-all | bytes 2097152 | tf_op jit(solution)/shard_map/all_to_all | solution.py:29
  90.5 0.0 copy-start.4
  90.5 0.0 all-gather.3.cloned.1.call-update
  90.6 0.2 reduce-scatter.2.cloned.1.call-start
  90.8 49.2 %all-gather.3.cloned.1.call-done = bf16[128,1,8,2048]{3,2,1,0:T(8,128)(2,1)} async-done(((bf16[128,1,8,512]{3,2,1,0:T(8,128)(2,1)}), bf16[128,1,8,2048]{3,2,1,0:T(8,128)(2,1)}) %all-gather.3.cloned.1.call-update) | async-done | bytes 4194320 | tf_op jit(solution)/shard_map/all_gather | solution.py:28
  140.0 0.0 copy-done.3
  140.0 0.0 copy-start.2
  140.0 3.6 %fusion.2 = f32[1024,256]{1,0:T(8,128)S(1)} fusion(bf16[128,1,8,2048]{3,2,1,0:T(8,128)(2,1)} %all-gather.3.cloned.1.call-done, bf16[1,2048,256]{2,1,0:T(8,128)(2,1)S(1)} %copy-done.3), kind=kOutput, calls=%fused_computation.5 | convolution fusion | flops 1073741824 | bytes 6291456 | tf_op jit(solution)/shard_map/dot_general | solution.py:36
  143.6 0.0 copy-done.4
  143.6 0.0 copy-done.2
  143.7 1.3 fusion.10
  145.0 0.0 copy-done
  145.0 3.2 %convert_bitcast_fusion = bf16[1,128,8,2048]{3,1,2,0:T(8,128)(2,1)} fusion(bf16[1,256,2048]{2,1,0:T(8,128)(2,1)S(1)} %copy-done, bf16[128,8,256]{2,1,0:T(8,128)(2,1)S(1)} %fusion.10), kind=kOutput, calls=%fused_computation.7 | convolution fusion | flops 1075838976 | bytes 5767168 | tf_op jit(solution)/shard_map/dot_general | solution.py:39
  148.2 0.0 copy-start.1
  148.2 0.0 reduce-scatter.2.cloned.1.call-update
  148.2 55.1 %reduce-scatter.2.cloned.1.call-done = bf16[1,128,8,512]{3,1,2,0:T(8,128)(2,1)} async-done(((bf16[1,128,8,2048]{3,1,2,0:T(8,128)(2,1)}), bf16[1,128,8,512]{3,1,2,0:T(8,128)(2,1)}) %reduce-scatter.2.cloned.1.call-update) | async-done | bytes 1048592 | tf_op jit(solution)/shard_map/reduce_scatter | solution.py:42
  203.3 2.8 copy.23
  206.1 16.6 %all-to-all-start.1 = ((bf16[1,128,8,512]{3,2,0,1:T(8,128)(2,1)}), bf16[1,128,8,512]{3,2,0,1:T(8,128)(2,1)S(1)}, u32[]{:S(2)}, u32[]{:S(2)}) async-start(bf16[1,128,8,512]{3,2,0,1:T(8,128)(2,1)} %copy.23), calls=%async_computation.2 | async-start | bytes 2097152 | tf_op jit(solution)/shard_map/all_to_all | solution.py:45
  222.7 0.0 copy-done.1
  222.7 0.1 copy.24
  222.8 54.2 %all-to-all-done.1 = bf16[1,128,8,512]{3,2,0,1:T(8,128)(2,1)S(1)} async-done(((bf16[1,128,8,512]{3,2,0,1:T(8,128)(2,1)}), bf16[1,128,8,512]{3,2,0,1:T(8,128)(2,1)S(1)}, u32[]{:S(2)}, u32[]{:S(2)}) %all-to-all-start.1) | async-done | bytes 1048608 | tf_op jit(solution)/shard_map/all_to_all | solution.py:45
  277.0 2.0 gather_fusion
  279.0 0.7 reshape.113
  279.7 2.1 multiply_reduce_fusion
  (10 shorter events, 0.1 us)
Async XLA Ops:
  6.5 138.4 %copy-start = (bf16[1,256,2048]{2,1,0:T(8,128)(2,1)S(1)}, bf16[1,256,2048]{2,1,0:T(8,128)(2,1)}, u32[]{:S(2)}) copy-start(bf16[1,256,2048]{2,1,0:T(8,128)(2,1)} %param.11) | copy-start | bytes 3145732
  6.5 133.5 %copy-start.3 = (bf16[1,2048,256]{2,1,0:T(8,128)(2,1)S(1)}, bf16[1,2048,256]{2,1,0:T(8,128)(2,1)}, u32[]{:S(2)}) copy-start(bf16[1,2048,256]{2,1,0:T(8,128)(2,1)} %param.9) | copy-start | bytes 3145732
  6.5 133.5 %all-gather.3.cloned.1.call-start = ((), (), s32[]{:S(2)}) async-start(), calls=%async_computation.4 | async-start | bytes 5242880 | tf_op jit(solution)/shard_map/all_gather | solution.py:28
  90.5 53.1 %copy-start.4 = (bf16[1,2048,256]{2,1,0:T(8,128)(2,1)S(1)}, bf16[1,2048,256]{2,1,0:T(8,128)(2,1)}, u32[]{:S(2)}) copy-start(bf16[1,2048,256]{2,1,0:T(8,128)(2,1)} %param.10) | copy-start | bytes 3145732
  90.6 112.8 %reduce-scatter.2.cloned.1.call-start = ((), (), s32[]{:S(2)}) async-start(), calls=%async_computation.3 | async-start | bytes 5242880 | tf_op jit(solution)/shard_map/reduce_scatter | solution.py:42
  140.0 3.6 %copy-start.2 = (bf16[128,1,8,2048]{3,2,1,0:T(8,128)(2,1)S(1)}, bf16[128,1,8,2048]{3,2,1,0:T(8,128)(2,1)}, u32[]{:S(2)}) copy-start(bf16[128,1,8,2048]{3,2,1,0:T(8,128)(2,1)} %all-gather.3.cloned.1.call-done) | copy-start | bytes 12582916
  148.2 74.5 %copy-start.1 = (f32[256,2]{0,1:T(2,128)S(1)}, f32[256,2]{0,1:T(2,128)}, u32[]{:S(2)}) copy-start(f32[256,2]{0,1:T(2,128)} %param.8) | copy-start | bytes 6148
  206.1 70.9 %all-to-all-start.1 = ((bf16[1,128,8,512]{3,2,0,1:T(8,128)(2,1)}), bf16[1,128,8,512]{3,2,0,1:T(8,128)(2,1)S(1)}, u32[]{:S(2)}, u32[]{:S(2)}) async-start(bf16[1,128,8,512]{3,2,0,1:T(8,128)(2,1)} %copy.23), calls=%async_computation.2 | async-start | bytes 2097152 | tf_op jit(solution)/shard_map/all_to_all | solution.py:45
Sparse Core Ops, SparseCore 0:
  90.7 49.3 all-gather.2
  148.3 54.9 reduce-scatter.1
where the time goes:
time: 290 us; the launch traced here: 289 us
  waiting for transfers between devices  159 us (55%)
  blocking collectives  74.7 us (26%)
  starting transfers between devices  16.8 us (6%)
  local copies, waits for them, and re-layouts  13.6 us (5%)
  between operations  13.6 us (5%)
  matrix products  8.07 us (3%)
  other arithmetic  3.26 us (1%)
    all_to_all x1, blocking collectives, body(): lax.all_to_all(send_buffer, 'dp', split_axis=0, concat_axis=1, tiled=True)  74.7 us
    reduce_scatter x1, waiting for transfers between devices, body(): lax.psum_scatter(partial_out.astype(jnp.bfloat16), 'tensor', scatter_dime...  55.1 us
    all_to_all x1, waiting for transfers between devices, body(): lax.all_to_all(reduced, 'dp', split_axis=1, concat_axis=0, tiled=True)  54.2 us
    all_gather x1, waiting for transfers between devices, body(): lax.all_gather(lax.all_to_all(send_buffer, 'dp', split_axis=0, concat_axi...  49.2 us
    all_to_all x1, starting transfers between devices, body(): lax.all_to_all(reduced, 'dp', split_axis=1, concat_axis=0, tiled=True)  16.6 us
    scatter x1, local copies, waits for them, and re-layouts, body(): send_buffer = jnp.zeros((experts_all * capacity, tokens.shape[1]), jnp.bf...  6.4 us
  transfers between devices with their start and end apart: 3, of which 3 were waited for; matrix products, arithmetic and copies ran while one was open for 0% of the time, Pallas kernels for 0%

commit v1 on v0

v1 whole, which is shorter than its diff:
```python
import jax
import jax.numpy as jnp
from jax import lax
from jax.experimental import pallas as pl
from jax.experimental.pallas import tpu as pltpu
from jax.sharding import PartitionSpec as P

MESH = pl.DeviceIdType.MESH
BF = jnp.bfloat16
F32 = jnp.float32
TOK = 256
WID = 512
CUT = 2
NEAR = 4
PAIRS = 8
FAR_ROWS = 224


def dot(a, b):
    return jnp.dot(a, b, preferred_element_type=F32)


def dot_t(a, b):
    return lax.dot_general(a, b, (((0,), (0,)), ((), ())), preferred_element_type=F32)


def kernel(
    tok, ids, rw, gate_hbm, up_hbm, down_hbm, out,
    TR, MO, MT, PK, FS, FR, F, Wg, Wu, Wd, ST, Hd, O, R, DI, FB, CB, CO, RA, RO,
    wl, zs, zr, ms, mr, fs, fr, ps, pr, ys, yr, hs, hr, ds, dr, qs, qr, bs, br, rs, rr,
):
    dp = lax.axis_index("dp")
    y = lax.axis_index("tensor")
    x, z, c = dp // 32, (dp // 2) % 16, dp % 2
    m = x * 2 + c

    def at(x1, z1, c1):
        return ((x1 * 16 + z1) * 2 + c1, y)

    def along_z(d, h):
        return at(x, (z + (h if d == 0 else 16 - h)) % 16, c)

    def in_plane(j):
        k = (m + j) % 8
        return k, at(k // 2, z, k % 2)

    y_next = [(dp, (y + 1) % 4), (dp, (y + 3) % 4)]
    sent = []

    def send(src, dst, s, r, dev):
        copy = pltpu.make_async_remote_copy(
            src_ref=src, dst_ref=dst, send_sem=s, recv_sem=r, device_id=dev, device_id_type=MESH
        )
        copy.start()
        sent.append(copy.wait_send)

    def got(dst, r):
        pltpu.make_async_copy(dst, dst, r).wait()

    def drain():
        while sent:
            sent.pop()()

    loads = [
        pltpu.make_async_copy(gate_hbm.at[0], Wg, wl.at[0]),
        pltpu.make_async_copy(up_hbm.at[0], Wu, wl.at[1]),
        pltpu.make_async_copy(down_hbm.at[0, :, pl.ds(pl.multiple_of(y * WID, WID), WID)], Wd.at[y], wl.at[2]),
    ]
    for load in loads:
        load.start()

    barrier = pltpu.get_barrier_semaphore()
    peers = [along_z(d, h) for d in (0, 1) for h in range(1, NEAR + 1)]
    peers += [in_plane(j)[1] for j in range(1, 8)] + y_next
    for dev in peers:
        pl.semaphore_signal(barrier, inc=1, device_id=dev, device_id_type=MESH)
    pl.semaphore_wait(barrier, len(peers))

    part = TOK // CUT

    def piece(ref, k):
        return ref.at[pl.ds(k * part, part)]

    def z_send(d, h, k):
        src = tok if h == 0 else TR.at[d, h - 1]
        send(piece(src, k), piece(TR.at[d, h], k), zs.at[d, h, k], zr.at[d, h, k], along_z(d, 1))

    for k in range(CUT):
        for d in (0, 1):
            z_send(d, 0, k)

    def columns(j):
        return pl.ds(pl.multiple_of(((y + j) % 4) * WID, WID), WID)

    for d in (0, 1):
        send(down_hbm.at[0, pl.ds(d * 128, 128), columns(2)], ST.at[d], ds.at[d], dr.at[d], y_next[d])
    for d in (0, 1):
        send(down_hbm.at[0, :, columns((1, 3)[d])], Wd.at[y], ds.at[2 + d], dr.at[2 + d], y_next[d])

    row = lax.broadcasted_iota(jnp.int32, (128, TOK), 0)
    hot = [(row == ids[k : k + 1, :]).astype(F32) for k in (0, 1)]
    before = (
        lax.broadcasted_iota(jnp.int32, (TOK, TOK), 0) < lax.broadcasted_iota(jnp.int32, (TOK, TOK), 1)
    ).astype(F32).astype(BF)
    count = [dot(hot[k].astype(BF), before) for k in (0, 1)]
    count[1] = count[1] + jnp.sum(hot[0], axis=1, keepdims=True)
    MO[...] = jnp.zeros((8, TOK), F32)
    for k in (0, 1):
        e = ids[k : k + 1, :]
        rank = jnp.sum(hot[k] * count[k], axis=0, keepdims=True)
        place = ((e >> 1) & 15) * 64 + ((e >> 5) * 2 + (e & 1)) * 8
        MO[k : k + 1, :] = place.astype(F32) + rank
        MO[2 + k : 3 + k, :] = rw[k : k + 1, :]
    for h in range(NEAR):
        for d in (0, 1):
            send(MO, MT.at[d, h], ms.at[d, h], mr.at[d, h], along_z(d, h + 1))

    def pair_target():
        r = lax.broadcasted_iota(jnp.int32, (128, TOK), 0)
        return (z * 64 + (r >> 4) * 8 + (r & 7)).astype(F32), (r >> 3) & 1

    def far_target(d):
        r = lax.broadcasted_iota(jnp.int32, (FAR_ROWS, TOK), 0)
        step = (r >> 6) + 1
        station = (z + (step if d == 0 else 16 - step)) & 15
        within = r & 63
        if d == 1:
            within = jnp.where(r >= 192, within + 32, within)
        return (station * 64 + within).astype(F32)

    def chosen(meta, target):
        return (meta[0:1, :] == target) | (meta[1:2, :] == target)

    def weights(meta, target, keep=None):
        w = jnp.where(meta[0:1, :] == target, meta[2:3, :], 0.0) + jnp.where(
            meta[1:2, :] == target, meta[3:4, :], 0.0
        )
        if keep is not None:
            w = jnp.where(keep, w, 0.0)
        high = w.astype(BF)
        return high, (w - high.astype(F32)).astype(BF)

    def mix(w, rows):
        return dot_t(w[0], rows) + dot_t(w[1], rows)

    def as_hot(mask):
        return jnp.where(mask, 1.0, 0.0).astype(BF)

    def select(meta, rows, d):
        target, side = pair_target()
        return dot(as_hot(chosen(meta, target) & (side == d)), rows)

    def to_plane(q):
        for j in range(1, 8):
            k, dev = in_plane(j)
            src = PK.at[q, pl.ds(pl.multiple_of(k * 16, 16), 16)]
            dst = F.at[q, y, pl.ds(pl.multiple_of(m * 16, 16), 16)]
            pltpu.make_async_remote_copy(
                src_ref=src, dst_ref=dst, send_sem=ps.at[q], recv_sem=pr.at[q], device_id=dev, device_id_type=MESH
            ).start()
        mine = pl.ds(pl.multiple_of(m * 16, 16), 16)
        F[q, y, mine, :] = PK[q, mine, :]
        sent.append(lambda: got(PK.at[q, pl.ds(0, 112)], ps.at[q]))

    def S0(q):
        if 1 <= q <= NEAR:
            pick = select(MT[0, q - 1], TR[0, q - 1], 0) + select(MT[1, q - 1], TR[1, q - 1], 1)
        else:
            r = lax.broadcasted_iota(jnp.int32, (128, 128), 0)
            k = lax.broadcasted_iota(jnp.int32, (128, 128), 1)
            slot, side = (r >> 4) * 8 + (r & 7), (r >> 3) & 1
            j = (q - 5) % 8
            if q:
                for d in (0, 1):
                    got(FR.at[j, pl.ds(d * 64, 64)], fr.at[d, j])
                pick = dot(as_hot(k == side * 64 + slot), FR[j])
            else:
                for d in (0, 1):
                    got(FR.at[j, pl.ds(d * 32, 32)], fr.at[d, j])
                pick = dot(as_hot((k == slot) & (side == 1)[:, :])[:, :64], FR[j, :64]) + PK[0].astype(F32)
        PK[q] = pick.astype(BF)
        to_plane(q)

    def gather_first(q, buf, s, r):
        for d in (0, 1):
            send(buf.at[q, y], buf.at[q, y], s.at[q, d], r.at[q, d], y_next[d])

    def gather_second(q, buf, s, r):
        for d in (0, 1):
            origin = (y + (3, 1)[d]) % 4
            got(buf.at[q, origin], r.at[q, d])
            half = buf.at[q, origin, pl.ds(d * 64, 64)]
            send(half, half, s.at[q, 2 + d], r.at[q, 2 + d], y_next[d])

    def gather_wait(q, buf, r):
        for d in (0, 1):
            got(buf.at[q, (y + 2) % 4, pl.ds(d * 64, 64)], r.at[q, 2 + d])

    def S1(q):
        got(F.at[q, y, pl.ds(0, 112)], pr.at[q])
        gather_first(q, F, ys, yr)

    def S2(q):
        gather_second(q, F, ys, yr)

    def S3(q):
        gather_wait(q, F, yr)
        g = jnp.zeros((128, 256), F32)
        u = jnp.zeros((128, 256), F32)
        for k in range(4):
            rows = F[q, k]
            g = g + dot(rows, Wg[k * WID : (k + 1) * WID, :])
            u = u + dot(rows, Wu[k * WID : (k + 1) * WID, :])
        Hd[q, y] = (g / (1.0 + jnp.exp(-g)) * u).astype(BF)

    def H(q):
        gather_first(q, Hd, hs, hr)

    def S4(q):
        gather_second(q, Hd, hs, hr)

    def S5(q):
        gather_wait(q, Hd, hr)
        o = jnp.zeros((128, WID), F32)
        for k in range(4):
            o = o + dot(Hd[q, k], Wd[k])
        O[q] = o.astype(BF)
        for j in range(1, 8):
            k, dev = in_plane(j)
            src = O.at[q, pl.ds(pl.multiple_of(k * 16, 16), 16)]
            dst = R.at[q, pl.ds(pl.multiple_of(m * 16, 16), 16)]
            pltpu.make_async_remote_copy(
                src_ref=src, dst_ref=dst, send_sem=qs.at[q], recv_sem=qr.at[q], device_id=dev, device_id_type=MESH
            ).start()
        mine = pl.ds(pl.multiple_of(m * 16, 16), 16)
        R[q, mine, :] = O[q, mine, :]
        sent.append(lambda: got(O.at[q, pl.ds(0, 112)], qs.at[q]))

    def S6(q):
        got(R.at[q, pl.ds(0, 112)], qr.at[q])
        if 1 <= q <= NEAR:
            target, side = pair_target()
            for d in (0, 1):
                CB[d, q - 1] = mix(weights(MT[d, q - 1], target, side == d), R[q])
            return
        k = lax.broadcasted_iota(jnp.int32, (128, 128), 0)
        r = lax.broadcasted_iota(jnp.int32, (128, 128), 1)
        slot, side = (r >> 4) * 8 + (r & 7), (r >> 3) & 1
        j = (q - 5) % 8
        DI[j] = dot(as_hot(k == side * 64 + slot), R[q]).astype(BF)
        for d in (0, 1):
            if q:
                rows, to = pl.ds(d * 64, 64), pl.ds(j * 64, 64)
            else:
                rows, to = pl.ds(64 + d * 32, 32), pl.ds(192, 32)
            send(DI.at[j, rows], FB.at[d, to], bs.at[d, j], br.at[d, j], along_z(1 - d, j + 1))

    def arrive(h, k):
        for d in (0, 1):
            got(piece(TR.at[d, h - 1], k), zr.at[d, h - 1, k])
            if h < NEAR:
                z_send(d, h, k)

    def round_of(h, between):
        arrive(h, 0)
        between()
        arrive(h, 1)
        for d in (0, 1):
            got(MT.at[d, h - 1], mr.at[d, h - 1])
        if h == NEAR:
            for d in (0, 1):
                FS[d] = dot(as_hot(chosen(MT[d, h - 1], far_target(d))), TR[d, h - 1]).astype(BF)
            for j in range(3, -1, -1):
                for d in (0, 1):
                    rows = pl.ds(j * 64, 64 if j < 3 else 32)
                    to = pl.ds(d * 64, 64) if j < 3 else pl.ds(d * 32, 32)
                    send(FS.at[d, rows], FR.at[j, to], fs.at[d, j], fr.at[d, j], along_z(d, j + 1))
        S0(h)

    PK[0] = select(MO[...], tok[...], 0).astype(BF)

    def forward_down():
        for d in (0, 1):
            got(ST.at[d], dr.at[d])
            send(ST.at[d], Wd.at[(y + (3, 1)[d]) % 4, pl.ds(d * 128, 128)], ds.at[4 + d], dr.at[4 + d], y_next[d])

    round_of(1, lambda: None)
    forward_down()
    round_of(2, lambda: S1(1))
    for load in loads:
        load.wait()
    round_of(3, lambda: S1(2))
    S2(1)
    round_of(4, lambda: S1(3))
    S2(2), S3(1)
    S0(5), S1(4), S2(3), S3(2)
    S0(6), S1(5), S2(4), S3(3)
    S0(7), S1(6), S2(5), S3(4)
    S0(0), S1(7), S2(6), S3(5), H(5)
    S1(0), S2(7), S3(6), H(6), S4(5)
    for d in (0, 1):
        got(Wd.at[(y + (3, 1)[d]) % 4], dr.at[2 + d])
        got(Wd.at[(y + 2) % 4, pl.ds(d * 128, 128)], dr.at[4 + d])
    S2(0), S3(7), H(7), S4(6), S5(5)
    S3(0), H(0), S4(7), S5(6), S6(5)
    H(4)
    S4(0), S5(7), S6(6)
    S4(4), H(3), H(2), H(1)
    S5(0), S6(7)
    S5(4), S6(0)
    S4(3), S6(4)
    S5(3), S4(2), S4(1)
    drain()

    def back(d, h, k, value):
        RO[d, h - 1, k * part : (k + 1) * part, :] = value.astype(BF)
        send(
            piece(RO.at[d, h - 1], k), piece(RA.at[d, h - 1], k), rs.at[d, h - 1, k], rr.at[d, h - 1, k], along_z(1 - d, 1)
        )

    for d in (0, 1):
        for j in range(4):
            to = pl.ds(j * 64, 64) if j < 3 else pl.ds(192, 32)
            got(FB.at[d, to], br.at[d, j])
        total = CB[d, NEAR - 1] + mix(weights(MT[d, NEAR - 1], far_target(d)), FB[d])
        for k in range(CUT):
            back(d, NEAR, k, total[k * part : (k + 1) * part])
    S6(3), S5(2), S5(1)

    def inwards(h):
        for k in range(CUT):
            for d in (0, 1):
                got(piece(RA.at[d, h], k), rr.at[d, h, k])
                rows = slice(k * part, (k + 1) * part)
                back(d, h, k, RA[d, h, rows, :].astype(F32) + CB[d, h - 1, rows, :])

    inwards(3)
    S6(2)
    inwards(2)
    S6(1)
    inwards(1)
    target, side = pair_target()
    CO[...] = mix(weights(MO[...], target, side == 0), R[0])
    drain()
    for k in range(CUT):
        for d in (0, 1):
            got(piece(RA.at[d, 0], k), rr.at[d, 0, k])
        rows = slice(k * part, (k + 1) * part)
        out[rows, :] = (
            CO[rows, :] + RA[0, 0, rows, :].astype(F32) + RA[1, 0, rows, :].astype(F32)
        ).astype(BF)


def body(tokens, expert_ids, route_weights, gate_weight, up_weight, down_weight):
    vmem = pl.BlockSpec(memory_space=pltpu.VMEM)
    hbm = pl.BlockSpec(memory_space=pl.ANY)
    V, DMA = pltpu.VMEM, pltpu.SemaphoreType.DMA
    scratch = [
        V((2, NEAR, TOK, WID), BF),
        V((8, TOK), F32),
        V((2, NEAR, 8, TOK), F32),
        V((PAIRS, 128, WID), BF),
        V((2, FAR_ROWS, WID), BF),
        V((4, 128, WID), BF),
        V((PAIRS, 4, 128, WID), BF),
        V((2048, 256), BF),
        V((2048, 256), BF),
        V((4, 256, WID), BF),
        V((2, 128, WID), BF),
        V((PAIRS, 4, 128, 256), BF),
        V((PAIRS, 128, WID), BF),
        V((PAIRS, 128, WID), BF),
        V((4, 128, WID), BF),
        V((2, FAR_ROWS, WID), BF),
        V((2, NEAR, TOK, WID), F32),
        V((TOK, WID), F32),
        V((2, NEAR, TOK, WID), BF),
        V((2, NEAR, TOK, WID), BF),
        DMA((3,)),
        DMA((2, NEAR, CUT)), DMA((2, NEAR, CUT)),
        DMA((2, NEAR)), DMA((2, NEAR)),
        DMA((2, 4)), DMA((2, 4)),
        DMA((PAIRS,)), DMA((PAIRS,)),
        DMA((PAIRS, 4)), DMA((PAIRS, 4)),
        DMA((PAIRS, 4)), DMA((PAIRS, 4)),
        DMA((6,)), DMA((6,)),
        DMA((PAIRS,)), DMA((PAIRS,)),
        DMA((2, 4)), DMA((2, 4)),
        DMA((2, NEAR, CUT)), DMA((2, NEAR, CUT)),
    ]
    return pl.pallas_call(
        kernel,
        out_shape=jax.ShapeDtypeStruct((TOK, WID), BF),
        in_specs=[vmem, vmem, vmem, hbm, hbm, hbm],
        out_specs=vmem,
        scratch_shapes=scratch,
        compiler_params=pltpu.CompilerParams(
            collective_id=0, has_side_effects=True, vmem_limit_bytes=48 * 1024 * 1024
        ),
        cost_estimate=pl.CostEstimate(
            flops=2 * 1024 * 3 * 2048 * 256, bytes_accessed=4 * 1024 * 1024, transcendentals=1024 * 256
        ),
    )(tokens, expert_ids.T, route_weights.T, gate_weight, up_weight, down_weight)


def solution(mesh):
    return jax.shard_map(
        body,
        mesh=mesh,
        in_specs=(
            P("dp", "tensor"),
            P("dp", None),
            P("dp", None),
            P("dp", None, "tensor"),
            P("dp", None, "tensor"),
            P("dp", "tensor", None),
        ),
        out_specs=P("dp", "tensor"),
        check_vma=False,
    )
```

time: 290 us -> 139 us (0.48)
  waiting for transfers between devices: 159 us -> 0 us
  Pallas kernels: 0 us -> 131 us
  blocking collectives: 74.7 us -> 0 us
  starting transfers between devices: 16.8 us -> 0 us
  between operations: 13.6 us -> 0.02 us
  matrix products: 8.07 us -> 0 us
  local copies, waits for them, and re-layouts: 13.6 us -> 6.69 us
  other arithmetic: 3.26 us -> 0 us
    pallas_call x0 -> x1, Pallas kernels: none -> 131 us  [body(): pl.pallas_call(kernel, out_shape=jax.ShapeDtypeStruct((TOK, WID), BF), in...]
    all_to_all x1 -> x0, blocking collectives: 74.7 us -> none  [body(): lax.all_to_all(send_buffer, 'dp', split_axis=0, concat_axis=1, tiled=True)]
    reduce_scatter x1 -> x0, waiting for transfers between devices: 55.1 us -> none  [body(): lax.psum_scatter(partial_out.astype(jnp.bfloat16), 'tensor', scatter_dime...]
    all_to_all x1 -> x0, waiting for transfers between devices: 54.2 us -> none  [body(): lax.all_to_all(reduced, 'dp', split_axis=1, concat_axis=0, tiled=True)]
    all_gather x1 -> x0, waiting for transfers between devices: 49.2 us -> none  [body(): lax.all_gather(lax.all_to_all(send_buffer, 'dp', split_axis=0, concat_axi...]
    all_to_all x1 -> x0, starting transfers between devices: 16.6 us -> none  [body(): lax.all_to_all(reduced, 'dp', split_axis=1, concat_axis=0, tiled=True)]
    dot_general x3 -> x0, matrix products: 8.07 us -> none  [the longest x1 3.59 us: body(): jnp.dot(token_rows, gate_weight[0], preferred_element_type=jnp.float32)]
    scatter x1 -> x0, local copies, waits for them, and re-layouts: 6.4 us -> none  [body(): send_buffer = jnp.zeros((experts_all * capacity, tokens.shape[1]), jnp.bf...]
  transfers between devices with their start and end apart: 3 -> 0, of which waited for: 3 -> 0; matrix products, arithmetic and copies ran while one was open for 0% -> 0% of each run, Pallas kernels for 0% -> 0%
where the time goes in v1:
time: 139 us; the launch traced here: 138 us
  Pallas kernels  131 us (94%)
  local copies, waits for them, and re-layouts  6.69 us (5%)
    pallas_call x1, Pallas kernels, body(): pl.pallas_call(kernel, out_shape=jax.ShapeDtypeStruct((TOK, WID), BF), in...  131 us
    unnamed x13, local copies, waits for them, and re-layouts  6.69 us

profile of v1, /device:TPU:1, one launch (start us, length us, event | category | flops | bytes accessed | tf_op | source)
XLA Modules:
  0.0 138.2 jit_solution(6779891359222274828)
XLA Ops:
  0.0 0.0 copy-start.4
  0.0 0.7 copy-done.4
  0.7 0.0 copy-start
  0.7 1.2 copy-done
  1.9 0.0 copy-start.1
  1.9 1.2 copy-done.1
  3.1 0.0 copy-start.2
  3.1 1.2 copy-done.2
  4.4 0.0 copy-start.3
  4.4 0.9 copy-done.3
  5.3 0.0 copy-start.5
  5.3 0.7 copy-done.5
  6.0 131.5 %shard_map.64 = bf16[256,512]{1,0:T(8,128)(2,1)S(1)} custom-call(bf16[256,512]{1,0:T(8,128)(2,1)S(1)} %copy-done.3, s32[2,256]{1,0:T(2,128)S(1)} %bitcast.2, f32[2,256]{1,0:T(2,128)S(1)} %bitcast.3, bf16[1,2048,256]{2,1,0:T(8,128)(2,1)S(1)} %copy-done, bf16[1,2048,256]{2,1,0:T(8,128)(2,1)S(1)} %copy-done.1, bf16[1,256,2048]{2,1,0:T(8,128)(2,1)S(1)} %copy-done.2), custom_call_target="tpu_custom_call" | custom-call | flops 3221225472 | bytes 4194304 | tf_op jit(solution)/shard_map/pallas_call | solution.py:391
  137.5 0.7 copy.8
Async XLA Ops:
  0.0 0.7 copy-start.4
  0.7 1.2 copy-start
  1.9 1.2 copy-start.1
  3.1 1.2 copy-start.2
  4.4 0.9 copy-start.3
  5.3 0.7 copy-start.5

commit v2 on v1

--- a/solution.py
+++ b/solution.py
@@ -261,21 +261,18 @@
             if h < NEAR:
                 z_send(d, h, k)
 
-    def round_of(h, between):
-        arrive(h, 0)
-        between()
-        arrive(h, 1)
+    def far_out():
+        for d in (0, 1):
+            FS[d] = dot(as_hot(chosen(MT[d, NEAR - 1], far_target(d))), TR[d, NEAR - 1]).astype(BF)
+        for j in range(4):
+            for d in (0, 1):
+                rows = pl.ds(j * 64, 64 if j < 3 else 32)
+                to = pl.ds(d * 64, 64) if j < 3 else pl.ds(d * 32, 32)
+                send(FS.at[d, rows], FR.at[j, to], fs.at[d, j], fr.at[d, j], along_z(d, j + 1))
+
+    def meta_of(h):
         for d in (0, 1):
             got(MT.at[d, h - 1], mr.at[d, h - 1])
-        if h == NEAR:
-            for d in (0, 1):
-                FS[d] = dot(as_hot(chosen(MT[d, h - 1], far_target(d))), TR[d, h - 1]).astype(BF)
-            for j in range(3, -1, -1):
-                for d in (0, 1):
-                    rows = pl.ds(j * 64, 64 if j < 3 else 32)
-                    to = pl.ds(d * 64, 64) if j < 3 else pl.ds(d * 32, 32)
-                    send(FS.at[d, rows], FR.at[j, to], fs.at[d, j], fr.at[d, j], along_z(d, j + 1))
-        S0(h)
 
     PK[0] = select(MO[...], tok[...], 0).astype(BF)
 
@@ -284,34 +281,26 @@
             got(ST.at[d], dr.at[d])
             send(ST.at[d], Wd.at[(y + (3, 1)[d]) % 4, pl.ds(d * 128, 128)], ds.at[4 + d], dr.at[4 + d], y_next[d])
 
-    round_of(1, lambda: None)
+    def down_there():
+        for load in loads:
+            load.wait()
+        for d in (0, 1):
+            got(Wd.at[(y + (3, 1)[d]) % 4], dr.at[2 + d])
+            got(Wd.at[(y + 2) % 4, pl.ds(d * 128, 128)], dr.at[4 + d])
+
+    arrive(1, 0), arrive(1, 1), meta_of(1), S0(1)
     forward_down()
-    round_of(2, lambda: S1(1))
-    for load in loads:
-        load.wait()
-    round_of(3, lambda: S1(2))
-    S2(1)
-    round_of(4, lambda: S1(3))
-    S2(2), S3(1)
-    S0(5), S1(4), S2(3), S3(2)
-    S0(6), S1(5), S2(4), S3(3)
-    S0(7), S1(6), S2(5), S3(4)
-    S0(0), S1(7), S2(6), S3(5), H(5)
-    S1(0), S2(7), S3(6), H(6), S4(5)
-    for d in (0, 1):
-        got(Wd.at[(y + (3, 1)[d]) % 4], dr.at[2 + d])
-        got(Wd.at[(y + 2) % 4, pl.ds(d * 128, 128)], dr.at[4 + d])
-    S2(0), S3(7), H(7), S4(6), S5(5)
-    S3(0), H(0), S4(7), S5(6), S6(5)
-    H(4)
-    S4(0), S5(7), S6(6)
-    S4(4), H(3), H(2), H(1)
-    S5(0), S6(7)
-    S5(4), S6(0)
-    S4(3), S6(4)
-    S5(3), S4(2), S4(1)
+    arrive(2, 0), S1(1), arrive(2, 1), meta_of(2), S0(2)
+    arrive(3, 0), S1(2), S2(1), arrive(3, 1), meta_of(3), S0(3)
+    arrive(4, 0), S1(3), S2(2), arrive(4, 1), meta_of(4), far_out(), S0(4)
+    down_there()
+    S2(3), S1(4), S0(5), S3(1), S3(2), S1(5), S0(6), S2(4), S3(3)
+    S1(6), S0(7), S2(5), S3(4), S1(7), S0(0), S2(6), S3(5), H(5)
+    S1(0), S2(7), S3(6), H(6), S4(5), S2(0), S3(7), H(7), S4(6), S5(5)
+    S3(0), H(0), S4(7), S5(6), S6(5), H(4), S4(0), S5(7), S6(6)
+    S4(4), H(3), H(2), H(1), S5(0), S6(7), S5(4), S6(0)
+    S4(3), S6(4), S5(3), S4(2), S4(1)
     drain()
-
     def back(d, h, k, value):
         RO[d, h - 1, k * part : (k + 1) * part, :] = value.astype(BF)
         send(
@@ -395,7 +384,7 @@
         out_specs=vmem,
         scratch_shapes=scratch,
         compiler_params=pltpu.CompilerParams(
-            collective_id=0, has_side_effects=True, vmem_limit_bytes=48 * 1024 * 1024
+            collective_id=0, has_side_effects=True, vmem_limit_bytes=60 * 1024 * 1024
         ),
         cost_estimate=pl.CostEstimate(
             flops=2 * 1024 * 3 * 2048 * 256, bytes_accessed=4 * 1024 * 1024, transcendentals=1024 * 256

time: 139 us -> 129 us (0.928)
  local copies, waits for them, and re-layouts: 6.69 us -> 1.67 us
  Pallas kernels: 131 us -> 127 us
    unnamed x13 -> x1, local copies, waits for them, and re-layouts: 6.69 us -> 1.67 us
    pallas_call x1, Pallas kernels: 131 us -> 127 us  [body(): pl.pallas_call(kernel, out_shape=jax.ShapeDtypeStruct((TOK, WID), BF), in...]
where the time goes in v2:
time: 129 us; the launch traced here: 128 us
  Pallas kernels  127 us (98%)
  local copies, waits for them, and re-layouts  1.67 us (1%)
    pallas_call x1, Pallas kernels, body(): pl.pallas_call(kernel, out_shape=jax.ShapeDtypeStruct((TOK, WID), BF), in...  127 us

profile of v2, /device:TPU:1, one launch (start us, length us, event | category | flops | bytes accessed | tf_op | source)
XLA Modules:
  0.0 128.4 jit_solution(17657512688780446312)
XLA Ops:
  0.0 126.7 %shard_map.64 = bf16[256,512]{1,0:T(8,128)(2,1)} custom-call(bf16[256,512]{1,0:T(8,128)(2,1)} %tok.1, s32[2,256]{1,0:T(2,128)} %bitcast.2, f32[2,256]{1,0:T(2,128)} %bitcast.3, bf16[1,2048,256]{2,1,0:T(8,128)(2,1)} %gate_hbm.1, bf16[1,2048,256]{2,1,0:T(8,128)(2,1)} %up_hbm.1, bf16[1,256,2048]{2,1,0:T(8,128)(2,1)} %down_hbm.1), custom_call_target="tpu_custom_call" | custom-call | flops 3221225472 | bytes 4194304 | tf_op jit(solution)/shard_map/pallas_call | solution.py:380
  126.7 1.7 %copy.8 = bf16[256,512]{1,0:T(8,128)(2,1)} copy(bf16[256,512]{1,0:T(8,128)(2,1)} %shard_map.64) | data formatting | bytes 524288

commit v3 on v2

--- a/solution.py
+++ b/solution.py
@@ -11,9 +11,24 @@
 TOK = 256
 WID = 512
 CUT = 2
-NEAR = 4
+OUT = 4
+BACK = 3
+NEAR = max(OUT, BACK)
 PAIRS = 8
-FAR_ROWS = 224
+
+
+def far_rows(near):
+    return 64 * (7 - near) + 32
+
+
+def far_index(q, near):
+    return q - near - 1 if q else 7 - near
+
+
+def far_slices(j, near, d):
+    if j < 7 - near:
+        return pl.ds(j * 64, 64), pl.ds(d * 64, 64)
+    return pl.ds(j * 64, 32), pl.ds(d * 32, 32)
 
 
 def dot(a, b):
@@ -70,7 +85,7 @@
         load.start()
 
     barrier = pltpu.get_barrier_semaphore()
-    peers = [along_z(d, h) for d in (0, 1) for h in range(1, NEAR + 1)]
+    peers = [along_z(d, h) for d in (0, 1) for h in range(1, 9 - min(OUT, BACK))]
     peers += [in_plane(j)[1] for j in range(1, 8)] + y_next
     for dev in peers:
         pl.semaphore_signal(barrier, inc=1, device_id=dev, device_id_type=MESH)
@@ -119,13 +134,13 @@
         r = lax.broadcasted_iota(jnp.int32, (128, TOK), 0)
         return (z * 64 + (r >> 4) * 8 + (r & 7)).astype(F32), (r >> 3) & 1
 
-    def far_target(d):
-        r = lax.broadcasted_iota(jnp.int32, (FAR_ROWS, TOK), 0)
+    def far_target(d, near):
+        r = lax.broadcasted_iota(jnp.int32, (far_rows(near), TOK), 0)
         step = (r >> 6) + 1
         station = (z + (step if d == 0 else 16 - step)) & 15
         within = r & 63
         if d == 1:
-            within = jnp.where(r >= 192, within + 32, within)
+            within = jnp.where(r >= 64 * (7 - near), within + 32, within)
         return (station * 64 + within).astype(F32)
 
     def chosen(meta, target):
@@ -163,13 +178,13 @@
         sent.append(lambda: got(PK.at[q, pl.ds(0, 112)], ps.at[q]))
 
     def S0(q):
-        if 1 <= q <= NEAR:
+        if 1 <= q <= OUT:
             pick = select(MT[0, q - 1], TR[0, q - 1], 0) + select(MT[1, q - 1], TR[1, q - 1], 1)
         else:
             r = lax.broadcasted_iota(jnp.int32, (128, 128), 0)
             k = lax.broadcasted_iota(jnp.int32, (128, 128), 1)
             slot, side = (r >> 4) * 8 + (r & 7), (r >> 3) & 1
-            j = (q - 5) % 8
+            j = far_index(q, OUT)
             if q:
                 for d in (0, 1):
                     got(FR.at[j, pl.ds(d * 64, 64)], fr.at[d, j])
@@ -238,7 +253,7 @@
 
     def S6(q):
         got(R.at[q, pl.ds(0, 112)], qr.at[q])
-        if 1 <= q <= NEAR:
+        if 1 <= q <= BACK:
             target, side = pair_target()
             for d in (0, 1):
                 CB[d, q - 1] = mix(weights(MT[d, q - 1], target, side == d), R[q])
@@ -246,28 +261,26 @@
         k = lax.broadcasted_iota(jnp.int32, (128, 128), 0)
         r = lax.broadcasted_iota(jnp.int32, (128, 128), 1)
         slot, side = (r >> 4) * 8 + (r & 7), (r >> 3) & 1
-        j = (q - 5) % 8
+        j = far_index(q, BACK)
         DI[j] = dot(as_hot(k == side * 64 + slot), R[q]).astype(BF)
         for d in (0, 1):
-            if q:
-                rows, to = pl.ds(d * 64, 64), pl.ds(j * 64, 64)
-            else:
-                rows, to = pl.ds(64 + d * 32, 32), pl.ds(192, 32)
+            to, rows = far_slices(j, BACK, d)
+            if not q:
+                rows = pl.ds(64 + d * 32, 32)
             send(DI.at[j, rows], FB.at[d, to], bs.at[d, j], br.at[d, j], along_z(1 - d, j + 1))
 
     def arrive(h, k):
         for d in (0, 1):
             got(piece(TR.at[d, h - 1], k), zr.at[d, h - 1, k])
-            if h < NEAR:
+            if h < OUT:
                 z_send(d, h, k)
 
     def far_out():
         for d in (0, 1):
-            FS[d] = dot(as_hot(chosen(MT[d, NEAR - 1], far_target(d))), TR[d, NEAR - 1]).astype(BF)
-        for j in range(4):
+            FS[d] = dot(as_hot(chosen(MT[d, OUT - 1], far_target(d, OUT))), TR[d, OUT - 1]).astype(BF)
+        for j in range(8 - OUT):
             for d in (0, 1):
-                rows = pl.ds(j * 64, 64 if j < 3 else 32)
-                to = pl.ds(d * 64, 64) if j < 3 else pl.ds(d * 32, 32)
+                rows, to = far_slices(j, OUT, d)
                 send(FS.at[d, rows], FR.at[j, to], fs.at[d, j], fr.at[d, j], along_z(d, j + 1))
 
     def meta_of(h):
@@ -295,12 +308,11 @@
     arrive(4, 0), S1(3), S2(2), arrive(4, 1), meta_of(4), far_out(), S0(4)
     down_there()
     S2(3), S1(4), S0(5), S3(1), S3(2), S1(5), S0(6), S2(4), S3(3)
-    S1(6), S0(7), S2(5), S3(4), S1(7), S0(0), S2(6), S3(5), H(5)
-    S1(0), S2(7), S3(6), H(6), S4(5), S2(0), S3(7), H(7), S4(6), S5(5)
-    S3(0), H(0), S4(7), S5(6), S6(5), H(4), S4(0), S5(7), S6(6)
-    S4(4), H(3), H(2), H(1), S5(0), S6(7), S5(4), S6(0)
-    S4(3), S6(4), S5(3), S4(2), S4(1)
-    drain()
+    S1(6), S0(7), S2(5), S3(4), S1(7), S0(0), S2(6), S3(5), H(4), H(5)
+    S1(0), S2(7), S3(6), H(6), S4(4), S4(5), S2(0), S3(7), H(7), S5(4), S4(6), S5(5)
+    S3(0), H(0), S4(7), S6(4), S5(6), S6(5), H(3), S4(0), S5(7), S6(6)
+    S4(3), H(2), H(1), S5(0), S6(7), S5(3), S6(0), S6(3)
+    S4(2), S4(1)
     def back(d, h, k, value):
         RO[d, h - 1, k * part : (k + 1) * part, :] = value.astype(BF)
         send(
@@ -308,13 +320,11 @@
         )
 
     for d in (0, 1):
-        for j in range(4):
-            to = pl.ds(j * 64, 64) if j < 3 else pl.ds(192, 32)
-            got(FB.at[d, to], br.at[d, j])
-        total = CB[d, NEAR - 1] + mix(weights(MT[d, NEAR - 1], far_target(d)), FB[d])
+        for j in range(8 - BACK):
+            got(FB.at[d, far_slices(j, BACK, d)[0]], br.at[d, j])
+        total = CB[d, BACK - 1] + mix(weights(MT[d, BACK - 1], far_target(d, BACK)), FB[d])
         for k in range(CUT):
-            back(d, NEAR, k, total[k * part : (k + 1) * part])
-    S6(3), S5(2), S5(1)
+            back(d, BACK, k, total[k * part : (k + 1) * part])
 
     def inwards(h):
         for k in range(CUT):
@@ -323,8 +333,7 @@
                 rows = slice(k * part, (k + 1) * part)
                 back(d, h, k, RA[d, h, rows, :].astype(F32) + CB[d, h - 1, rows, :])
 
-    inwards(3)
-    S6(2)
+    S5(2), S5(1), S6(2)
     inwards(2)
     S6(1)
     inwards(1)
@@ -345,12 +354,12 @@
     hbm = pl.BlockSpec(memory_space=pl.ANY)
     V, DMA = pltpu.VMEM, pltpu.SemaphoreType.DMA
     scratch = [
-        V((2, NEAR, TOK, WID), BF),
+        V((2, OUT, TOK, WID), BF),
         V((8, TOK), F32),
         V((2, NEAR, 8, TOK), F32),
         V((PAIRS, 128, WID), BF),
-        V((2, FAR_ROWS, WID), BF),
-        V((4, 128, WID), BF),
+        V((2, far_rows(OUT), WID), BF),
+        V((8 - OUT, 128, WID), BF),
         V((PAIRS, 4, 128, WID), BF),
         V((2048, 256), BF),
         V((2048, 256), BF),
@@ -359,23 +368,23 @@
         V((PAIRS, 4, 128, 256), BF),
         V((PAIRS, 128, WID), BF),
         V((PAIRS, 128, WID), BF),
-        V((4, 128, WID), BF),
-        V((2, FAR_ROWS, WID), BF),
-        V((2, NEAR, TOK, WID), F32),
+        V((8 - BACK, 128, WID), BF),
+        V((2, far_rows(BACK), WID), BF),
+        V((2, BACK, TOK, WID), F32),
         V((TOK, WID), F32),
-        V((2, NEAR, TOK, WID), BF),
-        V((2, NEAR, TOK, WID), BF),
+        V((2, BACK, TOK, WID), BF),
+        V((2, BACK, TOK, WID), BF),
         DMA((3,)),
-        DMA((2, NEAR, CUT)), DMA((2, NEAR, CUT)),
+        DMA((2, OUT, CUT)), DMA((2, OUT, CUT)),
         DMA((2, NEAR)), DMA((2, NEAR)),
-        DMA((2, 4)), DMA((2, 4)),
+        DMA((2, 8 - OUT)), DMA((2, 8 - OUT)),
         DMA((PAIRS,)), DMA((PAIRS,)),
         DMA((PAIRS, 4)), DMA((PAIRS, 4)),
         DMA((PAIRS, 4)), DMA((PAIRS, 4)),
         DMA((6,)), DMA((6,)),
         DMA((PAIRS,)), DMA((PAIRS,)),
-        DMA((2, 4)), DMA((2, 4)),
-        DMA((2, NEAR, CUT)), DMA((2, NEAR, CUT)),
+        DMA((2, 8 - BACK)), DMA((2, 8 - BACK)),
+        DMA((2, BACK, CUT)), DMA((2, BACK, CUT)),
     ]
     return pl.pallas_call(
         kernel,

time: 129 us -> 130 us (level)
    pallas_call x1, Pallas kernels: 127 us -> 128 us  [body(): pl.pallas_call(kernel, out_shape=jax.ShapeDtypeStruct((TOK, WID), BF), in...]
where the time goes in v3:
time: 130 us
  Pallas kernels  128 us (98%)
  local copies, waits for them, and re-layouts  1.67 us (1%)
    pallas_call x1, Pallas kernels, body(): pl.pallas_call(kernel, out_shape=jax.ShapeDtypeStruct((TOK, WID), BF), in...  128 us

profile of v3, /device:TPU:1, one launch (start us, length us, event | category | flops | bytes accessed | tf_op | source)
XLA Modules:
  0.0 129.7 jit_solution(17656832695760227084)
XLA Ops:
  0.0 128.1 %shard_map.64 = bf16[256,512]{1,0:T(8,128)(2,1)} custom-call(bf16[256,512]{1,0:T(8,128)(2,1)} %tok.1, s32[2,256]{1,0:T(2,128)} %bitcast.2, f32[2,256]{1,0:T(2,128)} %bitcast.3, bf16[1,2048,256]{2,1,0:T(8,128)(2,1)} %gate_hbm.1, bf16[1,2048,256]{2,1,0:T(8,128)(2,1)} %up_hbm.1, bf16[1,256,2048]{2,1,0:T(8,128)(2,1)} %down_hbm.1), custom_call_target="tpu_custom_call" | custom-call | flops 3221225472 | bytes 4194304 | tf_op jit(solution)/shard_map/pallas_call | solution.py:389
  128.1 1.7 %copy.8 = bf16[256,512]{1,0:T(8,128)(2,1)} copy(bf16[256,512]{1,0:T(8,128)(2,1)} %shard_map.64) | data formatting | bytes 524288
